TPU v7x, 128 devices: a whole 4x4x4 slice. The times are simulated.
128 devices in a mesh: trip: 8 (over x, core), exc: 16 (over y, z).
Axes of the slice: x: 4, y: 4, z: 4, core: 2. Of those that a mesh axis runs over, the one named last changes fastest.
Arguments:
- pes_grids: float32 [512, 16, 256], P(('trip', 'exc')), may hold values from -6 to 6
- modals: float32 [200, 128], P('trip'), may hold values from -1.8 to 1.8
- energies: float32 [200, 8], P('trip'), may hold values from 0.05 to 0.5
- triple_modes: int32 [512, 3], P(('trip', 'exc')), may hold values from 0 to 199, as said below
- routing: int32 [8, 16, 16], P('trip', None, 'exc'), may hold values from 0 to 3
- block_source: int32 [3072], P(('trip', 'exc')), may hold values from 0 to 15
- live_rows: int32 [3072], P(('trip', 'exc')), may hold values from 1 to 8
- trial_vectors: bfloat16 [3072, 512, 512], P(('trip', 'exc')), may hold values from -6 to 6
- spectator_energy: float32 [3072, 8], P(('trip', 'exc')), may hold values from 0.1 to 1
Outputs:
- sigma_blocks: bfloat16 [3072, 512, 512], P(('trip', 'exc'))
Inputs may be any that keep to these rules, and one draw needn't show every extreme that they name: `triple_modes`: the three modes of a triple are distinct.
All inputs are finite; a program needn't handle non-finite values.
Results may differ from a plain program's by a relative error of at most 0.005.
Values may be sent and summed in bfloat16 or wider, within the bound.
No kernel may reach another device: no remote copies, remote signals or barrier semaphores. Data moves between devices by JAX's collectives and lax.ppermute only.
A program may use at most 128 MiB of HBM per device.

v0:
```python
import jax
import jax.numpy as jnp
from jax import lax
from jax.experimental import pallas as pl
from jax.experimental.pallas import tpu as pltpu
from jax.sharding import PartitionSpec as P

NMOD = 8
G = 16
NVEC = 64
S = 512
HALF = 256
COLS = 16
TRIPS = 8
TABLE_ROWS = 40
MODAL_ROWS = 32
PAY_ROWS = 24
UNROLL = 12
F32 = jnp.float32
BF16 = jnp.bfloat16


def iota(shape, axis):
    return lax.broadcasted_iota(jnp.int32, shape, axis)


def pack_kernel(routing, triple_modes, pes, modals, energies, pay, table):
    lane = iota((8, HALF), 1)
    per = modals.shape[0]
    for q in range(COLS):
        local = routing[q]
        pay[q, 0:G, :] = pes[local]
        names = jnp.zeros((8, HALF), F32)
        for n in range(3):
            mode = triple_modes[local, n]
            owner = lax.div(mode, per)
            names = jnp.where(lane == n, owner.astype(F32), names)
            names = jnp.where(lane == 3 + n, (mode - owner * per).astype(F32), names)
        pay[q, G : G + 8, :] = names
    table[...] = jnp.zeros_like(table)
    table[0:per, :] = modals[...]
    table[MODAL_ROWS:TABLE_ROWS, 0:per] = energies[...]


def split(x):
    high = x.astype(BF16)
    return high, (x - high.astype(F32)).astype(BF16)


def pick(values, chosen):
    both = jnp.concatenate(split(values), axis=1)
    return jnp.dot(both, jnp.concatenate([chosen, chosen], axis=0), preferred_element_type=F32)


def ones_where(condition):
    return jnp.where(condition, 1.0, 0.0).astype(BF16)


def repeat_rows(x, count):
    rows, lanes = x.shape
    return jnp.broadcast_to(x[:, None, :], (rows, count, lanes)).reshape(rows * count, lanes)


def sigma_kernel(
    sources_live, pay, table_0, table_1, table_2, table_3, spectator, vectors, out,
    held, matrix, folded, summed, modal_j, modal_k, level, spread, used, order, in_sem, out_sem,
):
    blocks = held.shape[0]
    sources, live = sources_live.at[0], sources_live.at[1]

    def load(b):
        return pltpu.make_async_copy(vectors.at[b], held.at[b], in_sem.at[b])

    def store(b):
        return pltpu.make_async_copy(held.at[b], out.at[b], out_sem)

    for s in range(COLS):
        used[s] = 0

    @pl.loop(0, blocks)
    def _(b):
        used[sources[b]] = 1
        load(b).start()

    me = lax.axis_index("trip")


    def owner_of(slot):
        return (me ^ (slot & 3) ^ jnp.where((slot & 4) > 0, 6, 0)).astype(F32)

    owner = owner_of(iota((1, HALF), 1) // MODAL_ROWS)
    within = (iota((1, HALF), 1) % MODAL_ROWS).astype(F32)
    named = pay[:, G, :]
    owners = [named[:, n : n + 1] for n in range(3)]
    places = [named[:, n + 3 : n + 4] for n in range(3)]
    chosen = jnp.concatenate(
        [ones_where((owners[n] == owner) & (places[n] == within)) for n in range(3)], axis=0
    )
    tables = [
        table[n : n + TABLE_ROWS, :]
        for table in (table_0, table_1, table_2, table_3)
        for n in (0, TABLE_ROWS)
    ]
    modals = jnp.concatenate([table[0:MODAL_ROWS] for table in tables], axis=0)
    levels = jnp.concatenate([table[MODAL_ROWS:] for table in tables], axis=0)
    levels = jnp.concatenate([levels, jnp.zeros_like(levels)], axis=0)
    high, low = split(modals)
    rows = jnp.dot(chosen, high, preferred_element_type=F32) + jnp.dot(
        chosen, low, preferred_element_type=F32
    )
    own_modal = iota((128, 128), 1) // G == iota((128, 128), 0) % NMOD
    first, second, third = (
        jnp.where(own_modal, repeat_rows(rows[16 * n : 16 * n + 16], NMOD), 0.0)
        for n in range(3)
    )
    by_major = ones_where(iota((128, HALF), 1) // G == iota((128, HALF), 0) % G)
    by_minor = ones_where(iota((128, HALF), 1) % G == iota((128, HALF), 0) % G)
    modal_i = pick(first, by_minor[:, 0:128])
    part = iota((64, 128), 1) // G
    empty = jnp.zeros((128 - 3 * G, HALF), BF16)
    for n in range(COLS):
        mine = modal_i[8 * n : 8 * n + 8]
        high, low = split((mine[:, None, :] * mine[None, :, :]).reshape(64, 128))
        squares = jnp.where(part == 1, low.astype(F32), jnp.where(part < 3, high.astype(F32), 0.0))
        grid_high, grid_low = split(pay[n, 0:G, :])
        grids = jnp.concatenate([grid_high, grid_high, grid_low, empty], axis=0)
        summed[64 * n : 64 * n + 64, :] = jnp.dot(
            squares.astype(BF16), grids, preferred_element_type=F32
        )
    modal_j[...] = pick(second, by_major)
    modal_k[...] = pick(third, by_minor)
    level_high, level_low = split(levels)
    table_levels = jnp.concatenate([level_high, level_low], axis=0)
    lane = iota((1, 128), 1)
    level_owner = jnp.where(lane < 64, owner_of(lane // NMOD), -1.0)
    row, col = iota((128, 128), 0), iota((128, 128), 1)
    parts = []
    for n, digit in enumerate((col % 8, (col // 8) % 8, col % 8)):
        at = ones_where(places[n] == lane.astype(F32))
        found = lax.dot_general(
            at, table_levels, (((1,), (1,)), ((), ())), preferred_element_type=F32
        )
        own = jnp.where(owners[n] == level_owner, found[:, 0:128] + found[:, 128:256], 0.0)
        parts.append(pick(own, ones_where(row % NMOD == digit)))
    rest = parts[1] + parts[2]
    for a in range(NMOD):
        level[:, 128 * a : 128 * a + 128] = rest + parts[0][:, a : a + 1]
    padded = jnp.concatenate([spectator[...], jnp.zeros((blocks, 120), F32)], axis=1)
    spread[...] = pick(padded, ones_where(iota((128, S), 0) == iota((128, S), 1) // NVEC))

    on_left = iota((64, 128), 1) < 64
    on_diagonal = iota((64, 128), 1) % 64 == iota((64, 128), 0)
    combos = [(a, n) for a in range(NMOD) for n in range(a, NMOD)]
    place = {c: 64 * i for i, c in enumerate(combos)}
    place |= {(n, a): at for (a, n), at in place.items()}

    def build(s, spot):
        eight = pl.ds(pl.multiple_of(s * 8, 8), 8)
        pairs = (modal_j[eight, :][:, None, :] * modal_k[eight, :][None, :, :]).reshape(64, HALF)
        half = pairs.astype(BF16)
        weights = jnp.concatenate([half, half], axis=0)
        levels = level[pl.ds(s, 1), :]
        grids = [
            summed[pl.ds(pl.multiple_of(s * 64, 64) + a * NMOD, NMOD), :] for a in range(NMOD)
        ]
        scaled = [(grids[a][n : n + 1] * pairs).astype(BF16) for a, n in combos]
        whole = lax.dot_general(
            jnp.concatenate(scaled, axis=0),
            weights,
            (((1,), (1,)), ((), ())),
            preferred_element_type=F32,
        )
        for i, (a, n) in enumerate(combos):
            one = whole[64 * i : 64 * i + 64, :]
            if a == n:
                one = one + jnp.where(on_diagonal, levels[:, 128 * a : 128 * a + 128], 0.0)
            folded[spot, 64 * i : 64 * i + 64, :] = one.astype(BF16)

    def spread_out(s, spot):
        for a in range(NMOD):
            for j in range(NMOD // 2):
                even, odd = place[a, 2 * j], place[a, 2 * j + 1]
                matrix[s, j, 64 * a : 64 * a + 64, :] = jnp.where(
                    on_left, folded[spot, even : even + 64, :], folded[spot, odd : odd + 64, :]
                )

    count = jnp.int32(0)
    for s in range(COLS):
        order[count] = s
        count = count + used[s]
    order[count] = order[jnp.maximum(count - 1, 0)]

    @pl.loop(0, (count + 1) // 2)
    def _(step):
        here, there = order[2 * step], order[2 * step + 1]
        build(here, 0)
        build(there, 1)
        spread_out(here, 0)
        spread_out(there, 1)

    def product(b):
        whole = jnp.concatenate([matrix[sources[b], n] for n in range(4)], axis=1)
        return jnp.dot(whole, held[b], preferred_element_type=F32)

    def finish(b, block):
        scale = spread[pl.ds(b, 1), :]
        kept = ones_where(iota((1, S), 1) < live[b] * NVEC)
        held[b] = (block + scale * held[b].astype(F32)).astype(BF16) * kept
        store(b).start()

    @pl.loop(0, blocks // UNROLL)
    def _(step):
        first = step * UNROLL
        for n in range(UNROLL):
            load(first + n).wait()

        block = product(first)
        for n in range(UNROLL):
            later = product(first + n + 1) if n + 1 < UNROLL else None
            finish(first + n, block)
            block = later

    pltpu.make_async_copy(held, out, out_sem).wait()


def late_call(sources, live, received, tables, spectator, vectors):
    vmem, smem = pl.BlockSpec(memory_space=pltpu.VMEM), pl.BlockSpec(memory_space=pltpu.SMEM)
    anywhere = pl.BlockSpec(memory_space=pl.ANY)
    blocks = vectors.shape[0]
    return pl.pallas_call(
        sigma_kernel,
        out_shape=jax.ShapeDtypeStruct(vectors.shape, BF16),
        in_specs=[smem, vmem, vmem, vmem, vmem, vmem, vmem, anywhere],
        out_specs=anywhere,
        scratch_shapes=[
            pltpu.VMEM((blocks, S, S), BF16),
            pltpu.VMEM((COLS, 4, S, 128), BF16),
            pltpu.VMEM((2, 36 * 64, 128), BF16),
            pltpu.VMEM((COLS * 64, HALF), F32),
            pltpu.VMEM((128, HALF), F32),
            pltpu.VMEM((128, HALF), F32),
            pltpu.VMEM((COLS, 2 * S), F32),
            pltpu.VMEM((blocks, S), F32),
            pltpu.SMEM((COLS,), jnp.int32),
            pltpu.SMEM((COLS + 1,), jnp.int32),
            pltpu.SemaphoreType.DMA((blocks,)),
            pltpu.SemaphoreType.DMA,
        ],
        compiler_params=pltpu.CompilerParams(vmem_limit_bytes=48 * 2**20),
        cost_estimate=pl.CostEstimate(
            flops=2 * (blocks + COLS) * S**3, bytes_accessed=4 * blocks * S * S, transcendentals=0
        ),
    )(jnp.stack([sources, live]), received, *tables, spectator, vectors)


def on_device(
    pes_grids,
    modals,
    energies,
    triple_modes,
    routing,
    block_source,
    live_rows,
    trial_vectors,
    spectator_energy,
):
    vmem, smem = pl.BlockSpec(memory_space=pltpu.VMEM), pl.BlockSpec(memory_space=pltpu.SMEM)
    pay, table = pl.pallas_call(
        pack_kernel,
        out_shape=(
            jax.ShapeDtypeStruct((COLS, PAY_ROWS, HALF), F32),
            jax.ShapeDtypeStruct((TABLE_ROWS, 128), F32),
        ),
        in_specs=[smem, smem, vmem, vmem, vmem],
        out_specs=(vmem, vmem),
    )(routing.reshape(COLS), triple_modes, pes_grids, modals, energies.T)
    received = lax.all_to_all(pay, "exc", split_axis=0, concat_axis=0, tiled=True)

    def swap(x, step):
        return lax.ppermute(x, "trip", [(n, n ^ step) for n in range(TRIPS)])

    both = jnp.concatenate([table, swap(table, 1)], axis=0)
    near, far = swap(both, 2), swap(both, 6)
    tables = (both, near, far, swap(both, 4))
    return late_call(
        block_source, live_rows, received, tables, spectator_energy, trial_vectors
    )


def solution(mesh):
    in_specs = (
        P(("trip", "exc"), None, None),
        P("trip", None),
        P("trip", None),
        P(("trip", "exc"), None),
        P("trip", None, "exc"),
        P(("trip", "exc")),
        P(("trip", "exc")),
        P(("trip", "exc"), None, None),
        P(("trip", "exc"), None),
    )
    out_specs = P(("trip", "exc"), None, None)
    return jax.shard_map(
        on_device, mesh=mesh, in_specs=in_specs, out_specs=out_specs, check_vma=False
    )
```

profile of v0, /device:TPU:1, one launch (start us, length us, event | category | flops | bytes accessed | tf_op | source)
XLA Modules:
  0.0 35.9 jit_solution(13060187955715131262)
XLA Ops:
  0.0 1.8 %shard_map.91 = (f32[16,24,256]{2,1,0:T(8,128)}, f32[40,128]{1,0:T(8,128)}) custom-call(s32[16]{0:T(128)} %bitcast.5, s32[4,3]{1,0:T(4,128)} %triple_modes.1, f32[4,16,256]{2,1,0:T(8,128)} %pes.1, f32[25,128]{1,0:T(8,128)} %modals.1, f32[8,25]{1,0:T(8,128)} %bitcast.4), custom_call_target="tpu_custom_call" | custom-call | tf_op jit(solution)/shard_map/pallas_call | solution.py:268
  1.8 8.6 %all-to-all-start = ((f32[16,24,256]{2,1,0:T(8,128)}), f32[16,24,256]{2,1,0:T(8,128)S(1)}, u32[]{:S(2)}, u32[]{:S(2)}) async-start(f32[16,24,256]{2,1,0:T(8,128)} %get-tuple-element.7), calls=%async_computation | async-start | bytes 786432 | tf_op jit(solution)/shard_map/all_to_all | solution.py:277
  10.4 1.0 %collective-permute-start = (f32[40,128]{1,0:T(8,128)}, f32[40,128]{1,0:T(8,128)S(1)}, u32[]{:S(2)}, u32[]{:S(2)}) collective-permute-start(f32[40,128]{1,0:T(8,128)} %get-tuple-element.8), channel_id=1, source_target_pairs={{0,16},{16,0},{32,48},{48,32},{64,80},{80,64},{96,112},{112,96},{1... | collective-permute-start | bytes 61448 | tf_op jit(solution)/shard_map/ppermute | solution.py:280
  11.4 0.7 %constant_dynamic-update-slice_fusion.1 = f32[80,128]{1,0:T(8,128)S(1)} fusion(f32[40,128]{1,0:T(8,128)} %get-tuple-element.8), kind=kLoop, calls=%fused_computation.1 | loop fusion | bytes 40960
  12.2 0.3 collective-permute-done
  12.5 2.7 %collective-permute-start.3 = (f32[80,128]{1,0:T(8,128)S(1)}, f32[80,128]{1,0:T(8,128)S(1)}, u32[]{:S(2)}, u32[]{:S(2)}) collective-permute-start(f32[80,128]{1,0:T(8,128)S(1)} %constant_dynamic-update-slice_fusion.table_0), channel_id=1, source_target_pairs={{0,64},{16,80},{32,96},{48,112},{64,0},{80,16},{96,32},{112,48},{1... | collective-permute-start | bytes 122888 | tf_op jit(solution)/shard_map/ppermute | solution.py:280
  15.2 0.9 %collective-permute-start.2 = (f32[80,128]{1,0:T(8,128)S(1)}, f32[80,128]{1,0:T(8,128)S(1)}, u32[]{:S(2)}, u32[]{:S(2)}) collective-permute-start(f32[80,128]{1,0:T(8,128)S(1)} %constant_dynamic-update-slice_fusion.table_0), channel_id=1, source_target_pairs={{0,96},{16,112},{32,64},{48,80},{64,32},{80,48},{96,0},{112,16},{1... | collective-permute-start | bytes 122888 | tf_op jit(solution)/shard_map/ppermute | solution.py:280
  16.1 0.0 collective-permute-start.1
  16.1 0.7 %pad_add_fusion.sources_live = s32[2,24]{1,0:T(2,128)S(1)} fusion(s32[1,24]{1,0:T(1,128)} %bitcast.6, s32[1,24]{1,0:T(1,128)} %bitcast.7), kind=kLoop, calls=%fused_computation.2 | loop fusion | flops 48 | bytes 384 | tf_op jit(solution)/shard_map/stack | solution.py:253
  16.8 0.8 %copy.10.spectator = f32[24,8]{1,0:T(8,128)S(1)} copy(f32[24,8]{0,1:T(8,128)} %param.17) | data formatting | bytes 1536 | tf_op args[8]
  17.5 0.0 collective-permute-done.3.table_3
  17.6 2.1 %collective-permute-done.2.table_2 = f32[80,128]{1,0:T(8,128)S(1)} collective-permute-done((f32[80,128]{1,0:T(8,128)S(1)}, f32[80,128]{1,0:T(8,128)S(1)}, u32[]{:S(2)}, u32[]{:S(2)}) %collective-permute-start.2) | collective-permute-done | bytes 40992 | tf_op jit(solution)/shard_map/ppermute | solution.py:280
  19.6 0.0 collective-permute-done.1.table_1
  19.6 0.0 all-to-all-done.pay
  19.6 16.3 %shard_map.92 = bf16[24,512,512]{2,1,0:T(8,128)(2,1)} custom-call(s32[2,24]{1,0:T(2,128)S(1)} %pad_add_fusion.sources_live, f32[16,24,256]{2,1,0:T(8,128)S(1)} %all-to-all-done.pay, f32[80,128]{1,0:T(8,128)S(1)} %constant_dynamic-update-slice_fusion.table_0, f32[80,128]{1,0:T(8,128)S(1)} %collective-permute-done.1.table_1, ...), custom_call_target="tpu_custom_call" | custom-call | flops 10737418240 | bytes 25165824 | tf_op jit(solution)/shard_map/pallas_call | solution.py:230
  (1 shorter events, 0.0 us)
Async XLA Ops:
  1.8 17.8 %all-to-all-start = ((f32[16,24,256]{2,1,0:T(8,128)}), f32[16,24,256]{2,1,0:T(8,128)S(1)}, u32[]{:S(2)}, u32[]{:S(2)}) async-start(f32[16,24,256]{2,1,0:T(8,128)} %get-tuple-element.7), calls=%async_computation | async-start | bytes 786432 | tf_op jit(solution)/shard_map/all_to_all | solution.py:277
  10.4 2.1 %collective-permute-start = (f32[40,128]{1,0:T(8,128)}, f32[40,128]{1,0:T(8,128)S(1)}, u32[]{:S(2)}, u32[]{:S(2)}) collective-permute-start(f32[40,128]{1,0:T(8,128)} %get-tuple-element.8), channel_id=1, source_target_pairs={{0,16},{16,0},{32,48},{48,32},{64,80},{80,64},{96,112},{112,96},{1... | collective-permute-start | bytes 61448 | tf_op jit(solution)/shard_map/ppermute | solution.py:280
  12.5 5.1 %collective-permute-start.3 = (f32[80,128]{1,0:T(8,128)S(1)}, f32[80,128]{1,0:T(8,128)S(1)}, u32[]{:S(2)}, u32[]{:S(2)}) collective-permute-start(f32[80,128]{1,0:T(8,128)S(1)} %constant_dynamic-update-slice_fusion.table_0), channel_id=1, source_target_pairs={{0,64},{16,80},{32,96},{48,112},{64,0},{80,16},{96,32},{112,48},{1... | collective-permute-start | bytes 122888 | tf_op jit(solution)/shard_map/ppermute | solution.py:280
  15.2 4.4 %collective-permute-start.2 = (f32[80,128]{1,0:T(8,128)S(1)}, f32[80,128]{1,0:T(8,128)S(1)}, u32[]{:S(2)}, u32[]{:S(2)}) collective-permute-start(f32[80,128]{1,0:T(8,128)S(1)} %constant_dynamic-update-slice_fusion.table_0), channel_id=1, source_target_pairs={{0,96},{16,112},{32,64},{48,80},{64,32},{80,48},{96,0},{112,16},{1... | collective-permute-start | bytes 122888 | tf_op jit(solution)/shard_map/ppermute | solution.py:280
  16.1 3.5 %collective-permute-start.1 = (f32[80,128]{1,0:T(8,128)S(1)}, f32[80,128]{1,0:T(8,128)S(1)}, u32[]{:S(2)}, u32[]{:S(2)}) collective-permute-start(f32[80,128]{1,0:T(8,128)S(1)} %constant_dynamic-update-slice_fusion.table_0), channel_id=1, source_target_pairs={{0,32},{16,48},{32,0},{48,16},{64,96},{80,112},{96,64},{112,80},{1... | collective-permute-start | bytes 122888 | tf_op jit(solution)/shard_map/ppermute | solution.py:280
where the time goes:
time: 36.4 us; the launch traced here: 35.9 us
  Pallas kernels  18.1 us (50%)
  starting transfers between devices  13.2 us (36%)
  waiting for transfers between devices  2.38 us (7%)
  local copies, waits for them, and re-layouts  1.49 us (4%)
  other arithmetic  0.68 us (2%)
    pallas_call x1, Pallas kernels, late_call(): pl.pallas_call(sigma_kernel, out_shape=jax.ShapeDtypeStruct(vectors.shape...  16.3 us
    all_to_all x1, starting transfers between devices, on_device(): lax.all_to_all(pay, 'exc', split_axis=0, concat_axis=0, tiled=True)  8.6 us
    ppermute x4, starting transfers between devices, swap(): return lax.ppermute(x, 'trip', [(n, n ^ step) for n in range(TRIPS)])  4.64 us
    ppermute x4, waiting for transfers between devices, swap(): return lax.ppermute(x, 'trip', [(n, n ^ step) for n in range(TRIPS)])  2.38 us
    pallas_call x1, Pallas kernels, on_device(): pl.pallas_call(pack_kernel, out_shape=(jax.ShapeDtypeStruct((COLS, PAY_RO...  1.8 us
    unnamed x2, local copies, waits for them, and re-layouts  1.49 us
  transfers between devices with their start and end apart: 5, of which 2 were waited for; matrix products, arithmetic and copies ran while one was open for 6% of the time, Pallas kernels for 0%

commit v1 on v0

--- a/solution.py
+++ b/solution.py
@@ -24,22 +24,31 @@
     return lax.broadcasted_iota(jnp.int32, shape, axis)
 
 
-def pack_kernel(routing, triple_modes, pes, modals, energies, pay, table):
+def pack_kernel(routing, triple_modes, pes, modals, energies, pay, table, names_of, sems):
     lane = iota((8, HALF), 1)
     per = modals.shape[0]
+
+    def grids(q, local):
+        return pltpu.make_async_copy(pes.at[local], pay.at[q, pl.ds(0, G), :], sems.at[q])
+
+    naming = pltpu.make_async_copy(names_of, pay.at[:, pl.ds(G, 8), :], sems.at[COLS])
     for q in range(COLS):
         local = routing[q]
-        pay[q, 0:G, :] = pes[local]
+        grids(q, local).start()
         names = jnp.zeros((8, HALF), F32)
         for n in range(3):
             mode = triple_modes[local, n]
             owner = lax.div(mode, per)
             names = jnp.where(lane == n, owner.astype(F32), names)
             names = jnp.where(lane == 3 + n, (mode - owner * per).astype(F32), names)
-        pay[q, G : G + 8, :] = names
+        names_of[q] = names
+    naming.start()
     table[...] = jnp.zeros_like(table)
     table[0:per, :] = modals[...]
     table[MODAL_ROWS:TABLE_ROWS, 0:per] = energies[...]
+    for q in range(COLS):
+        grids(q, 0).wait()
+    naming.wait()
 
 
 def split(x):
@@ -271,8 +280,12 @@
             jax.ShapeDtypeStruct((COLS, PAY_ROWS, HALF), F32),
             jax.ShapeDtypeStruct((TABLE_ROWS, 128), F32),
         ),
-        in_specs=[smem, smem, vmem, vmem, vmem],
-        out_specs=(vmem, vmem),
+        in_specs=[smem, smem, pl.BlockSpec(memory_space=pl.ANY), vmem, vmem],
+        out_specs=(pl.BlockSpec(memory_space=pl.ANY), vmem),
+        scratch_shapes=[
+            pltpu.VMEM((COLS, 8, HALF), F32),
+            pltpu.SemaphoreType.DMA((COLS + 1,)),
+        ],
     )(routing.reshape(COLS), triple_modes, pes_grids, modals, energies.T)
     received = lax.all_to_all(pay, "exc", split_axis=0, concat_axis=0, tiled=True)
 

time: 36.4 us -> 45.5 us (1.25)
  the two profiles are of different devices: /device:TPU:1 before, /device:TPU:8 now
where the time goes in v1:
time: 45.5 us; the launch traced here: 44.9 us
  Pallas kernels  26.8 us (59%)
  starting transfers between devices  12.6 us (28%)
  waiting for transfers between devices  3.29 us (7%)
  local copies, waits for them, and re-layouts  1.49 us (3%)
  other arithmetic  0.68 us (1%)
    pallas_call x1, Pallas kernels, late_call(): pl.pallas_call(sigma_kernel, out_shape=jax.ShapeDtypeStruct(vectors.shape...  16.3 us
    pallas_call x1, Pallas kernels, on_device(): pl.pallas_call(pack_kernel, out_shape=(jax.ShapeDtypeStruct((COLS, PAY_RO...  10.5 us
    all_to_all x1, starting transfers between devices, on_device(): lax.all_to_all(pay, 'exc', split_axis=0, concat_axis=0, tiled=True)  8.42 us
    ppermute x4, starting transfers between devices, swap(): return lax.ppermute(x, 'trip', [(n, n ^ step) for n in range(TRIPS)])  4.17 us
    ppermute x4, waiting for transfers between devices, swap(): return lax.ppermute(x, 'trip', [(n, n ^ step) for n in range(TRIPS)])  3.29 us
    unnamed x2, local copies, waits for them, and re-layouts  1.49 us
  transfers between devices with their start and end apart: 5, of which 2 were waited for; matrix products, arithmetic and copies ran while one was open for 5% of the time, Pallas kernels for 0%

profile of v1, /device:TPU:8, one launch (start us, length us, event | category | flops | bytes accessed | tf_op | source)
XLA Modules:
  0.0 44.9 jit_solution(3589478282036278848)
XLA Ops:
  0.0 10.5 %shard_map.91 = (f32[16,24,256]{2,1,0:T(8,128)}, f32[40,128]{1,0:T(8,128)}) custom-call(s32[16]{0:T(128)} %bitcast.5, s32[4,3]{1,0:T(4,128)} %triple_modes.1, f32[4,16,256]{2,1,0:T(8,128)} %pes.1, f32[25,128]{1,0:T(8,128)} %modals.1, f32[8,25]{1,0:T(8,128)} %bitcast.4), custom_call_target="tpu_custom_call" | custom-call | tf_op jit(solution)/shard_map/pallas_call | solution.py:277
  10.5 8.4 %all-to-all-start = ((f32[16,24,256]{2,1,0:T(8,128)}), f32[16,24,256]{2,1,0:T(8,128)S(1)}, u32[]{:S(2)}, u32[]{:S(2)}) async-start(f32[16,24,256]{2,1,0:T(8,128)} %get-tuple-element.7), calls=%async_computation | async-start | bytes 786432 | tf_op jit(solution)/shard_map/all_to_all | solution.py:290
  19.0 0.0 collective-permute-start
  19.0 0.7 %constant_dynamic-update-slice_fusion.1 = f32[80,128]{1,0:T(8,128)S(1)} fusion(f32[40,128]{1,0:T(8,128)} %get-tuple-element.8), kind=kLoop, calls=%fused_computation.1 | loop fusion | bytes 40960
  19.7 0.7 %collective-permute-done = f32[40,128]{1,0:T(8,128)S(1)} collective-permute-done((f32[40,128]{1,0:T(8,128)}, f32[40,128]{1,0:T(8,128)S(1)}, u32[]{:S(2)}, u32[]{:S(2)}) %collective-permute-start) | collective-permute-done | bytes 20512 | tf_op jit(solution)/shard_map/ppermute | solution.py:293
  20.4 3.0 %collective-permute-start.3 = (f32[80,128]{1,0:T(8,128)S(1)}, f32[80,128]{1,0:T(8,128)S(1)}, u32[]{:S(2)}, u32[]{:S(2)}) collective-permute-start(f32[80,128]{1,0:T(8,128)S(1)} %constant_dynamic-update-slice_fusion.table_0), channel_id=1, source_target_pairs={{0,64},{16,80},{32,96},{48,112},{64,0},{80,16},{96,32},{112,48},{1... | collective-permute-start | bytes 122888 | tf_op jit(solution)/shard_map/ppermute | solution.py:293
  23.4 1.1 %collective-permute-start.2 = (f32[80,128]{1,0:T(8,128)S(1)}, f32[80,128]{1,0:T(8,128)S(1)}, u32[]{:S(2)}, u32[]{:S(2)}) collective-permute-start(f32[80,128]{1,0:T(8,128)S(1)} %constant_dynamic-update-slice_fusion.table_0), channel_id=1, source_target_pairs={{0,96},{16,112},{32,64},{48,80},{64,32},{80,48},{96,0},{112,16},{1... | collective-permute-start | bytes 122888 | tf_op jit(solution)/shard_map/ppermute | solution.py:293
  24.5 0.0 collective-permute-start.1
  24.5 0.7 %pad_add_fusion.sources_live = s32[2,24]{1,0:T(2,128)S(1)} fusion(s32[1,24]{1,0:T(1,128)} %bitcast.6, s32[1,24]{1,0:T(1,128)} %bitcast.7), kind=kLoop, calls=%fused_computation.2 | loop fusion | flops 48 | bytes 384 | tf_op jit(solution)/shard_map/stack | solution.py:262
  25.2 0.8 %copy.10.spectator = f32[24,8]{1,0:T(8,128)S(1)} copy(f32[24,8]{0,1:T(8,128)} %param.17) | data formatting | bytes 1536 | tf_op args[8]
  26.0 0.0 collective-permute-done.3.table_3
  26.0 2.6 %collective-permute-done.2.table_2 = f32[80,128]{1,0:T(8,128)S(1)} collective-permute-done((f32[80,128]{1,0:T(8,128)S(1)}, f32[80,128]{1,0:T(8,128)S(1)}, u32[]{:S(2)}, u32[]{:S(2)}) %collective-permute-start.2) | collective-permute-done | bytes 40992 | tf_op jit(solution)/shard_map/ppermute | solution.py:293
  28.6 0.0 collective-permute-done.1.table_1
  28.6 0.0 all-to-all-done.pay
  28.6 16.3 %shard_map.92 = bf16[24,512,512]{2,1,0:T(8,128)(2,1)} custom-call(s32[2,24]{1,0:T(2,128)S(1)} %pad_add_fusion.sources_live, f32[16,24,256]{2,1,0:T(8,128)S(1)} %all-to-all-done.pay, f32[80,128]{1,0:T(8,128)S(1)} %constant_dynamic-update-slice_fusion.table_0, f32[80,128]{1,0:T(8,128)S(1)} %collective-permute-done.1.table_1, ...), custom_call_target="tpu_custom_call" | custom-call | flops 10737418240 | bytes 25165824 | tf_op jit(solution)/shard_map/pallas_call | solution.py:239
  (1 shorter events, 0.0 us)
Async XLA Ops:
  10.5 18.1 %all-to-all-start = ((f32[16,24,256]{2,1,0:T(8,128)}), f32[16,24,256]{2,1,0:T(8,128)S(1)}, u32[]{:S(2)}, u32[]{:S(2)}) async-start(f32[16,24,256]{2,1,0:T(8,128)} %get-tuple-element.7), calls=%async_computation | async-start | bytes 786432 | tf_op jit(solution)/shard_map/all_to_all | solution.py:290
  19.0 1.4 %collective-permute-start = (f32[40,128]{1,0:T(8,128)}, f32[40,128]{1,0:T(8,128)S(1)}, u32[]{:S(2)}, u32[]{:S(2)}) collective-permute-start(f32[40,128]{1,0:T(8,128)} %get-tuple-element.8), channel_id=1, source_target_pairs={{0,16},{16,0},{32,48},{48,32},{64,80},{80,64},{96,112},{112,96},{1... | collective-permute-start | bytes 61448 | tf_op jit(solution)/shard_map/ppermute | solution.py:293
  20.4 5.6 %collective-permute-start.3 = (f32[80,128]{1,0:T(8,128)S(1)}, f32[80,128]{1,0:T(8,128)S(1)}, u32[]{:S(2)}, u32[]{:S(2)}) collective-permute-start(f32[80,128]{1,0:T(8,128)S(1)} %constant_dynamic-update-slice_fusion.table_0), channel_id=1, source_target_pairs={{0,64},{16,80},{32,96},{48,112},{64,0},{80,16},{96,32},{112,48},{1... | collective-permute-start | bytes 122888 | tf_op jit(solution)/shard_map/ppermute | solution.py:293
  23.4 5.2 %collective-permute-start.2 = (f32[80,128]{1,0:T(8,128)S(1)}, f32[80,128]{1,0:T(8,128)S(1)}, u32[]{:S(2)}, u32[]{:S(2)}) collective-permute-start(f32[80,128]{1,0:T(8,128)S(1)} %constant_dynamic-update-slice_fusion.table_0), channel_id=1, source_target_pairs={{0,96},{16,112},{32,64},{48,80},{64,32},{80,48},{96,0},{112,16},{1... | collective-permute-start | bytes 122888 | tf_op jit(solution)/shard_map/ppermute | solution.py:293
  24.5 4.1 %collective-permute-start.1 = (f32[80,128]{1,0:T(8,128)S(1)}, f32[80,128]{1,0:T(8,128)S(1)}, u32[]{:S(2)}, u32[]{:S(2)}) collective-permute-start(f32[80,128]{1,0:T(8,128)S(1)} %constant_dynamic-update-slice_fusion.table_0), channel_id=1, source_target_pairs={{0,32},{16,48},{32,0},{48,16},{64,96},{80,112},{96,64},{112,80},{1... | collective-permute-start | bytes 122888 | tf_op jit(solution)/shard_map/ppermute | solution.py:293
